TPU v7x, 32 devices: a whole 2x2x4 slice. The times are simulated.
32 devices in a mesh: lat: 4 (over x, core), items: 8 (over z, y).
Axes of the slice: x: 2, y: 2, z: 4, core: 2. Of those that a mesh axis runs over, the one named last changes fastest.
Arguments:
- tokens: bfloat16 [24, 2, 8, 16, 512], P('items', None, 'lat'), may hold values from -6 to 6
- norm1_gain: bfloat16 [512], replicated, may hold values from 0.5 to 1.5
- norm1_bias: bfloat16 [512], replicated, may hold values from -1 to 1
- qkv_weight: bfloat16 [512, 1536], replicated, may hold values from -0.25 to 0.25
- qv_bias: bfloat16 [2, 512], replicated, may hold values from -1 to 1
- proj_weight: bfloat16 [512, 512], replicated, may hold values from -0.75 to 0.75
- proj_bias: bfloat16 [512], replicated, may hold values from -1 to 1
- norm2_gain: bfloat16 [512], replicated, may hold values from 0.5 to 1.5
- norm2_bias: bfloat16 [512], replicated, may hold values from -1 to 1
- fc1_weight: bfloat16 [512, 2048], replicated, may hold values from -0.25 to 0.25
- fc1_bias: bfloat16 [2048], replicated, may hold values from -1 to 1
- fc2_weight: bfloat16 [2048, 512], replicated, may hold values from -0.125 to 0.125
- fc2_bias: bfloat16 [512], replicated, may hold values from -1 to 1
- cotangent: bfloat16 [24, 2, 8, 16, 512], P('items', None, 'lat'), may hold values from -6 to 6
Outputs:
- mixed: bfloat16 [24, 2, 8, 16, 512], P('items', None, 'lat')
- tokens_grad: bfloat16 [24, 2, 8, 16, 512], P('items', None, 'lat')
- norm1_gain_grad: float32 [512], replicated
- norm1_bias_grad: float32 [512], replicated
- qkv_weight_grad: float32 [512, 1536], replicated
- qv_bias_grad: float32 [2, 512], replicated
- proj_weight_grad: float32 [512, 512], replicated
- proj_bias_grad: float32 [512], replicated
- norm2_gain_grad: float32 [512], replicated
- norm2_bias_grad: float32 [512], replicated
- fc1_weight_grad: float32 [512, 2048], replicated
- fc1_bias_grad: float32 [2048], replicated
- fc2_weight_grad: float32 [2048, 512], replicated
- fc2_bias_grad: float32 [512], replicated
All inputs are finite; a program needn't handle non-finite values.
Results may differ from a plain program's by a relative error of at most 0.012.
Values may be sent and summed in bfloat16 or wider, within the bound.
No kernel may reach another device: no remote copies, remote signals or barrier semaphores. Data moves between devices by JAX's collectives and lax.ppermute only.
A program may use at most 128 MiB of HBM per device.

v0:
```python
import jax
import jax.numpy as jnp
from jax import lax
from jax.sharding import PartitionSpec as P

HEADS = 16
HEAD_DIM = 32
STEPS = 2
LON = 16
ROW_REACH = 1
COL_REACH = 2
epsilon = 1e-06


def padded(block, sides, width):
    for axis, dim in sides:
        count = lax.axis_size(axis)
        forward = [(i, i + 1) for i in range(count - 1)]
        backward = [(target, source) for source, target in forward]
        low = lax.ppermute(
            lax.slice_in_dim(block, block.shape[dim] - width, None, axis=dim), axis, forward
        )
        high = lax.ppermute(lax.slice_in_dim(block, 0, width, axis=dim), axis, backward)
        block = jnp.concatenate([low, block, high], axis=dim)
    return block


def shifted_2(block, axis, distance):
    devices = range(lax.axis_size(axis))
    route = [(i - distance, i) for i in devices if i - distance in devices]
    return lax.ppermute(block, axis, route)


def layer_norm(values, gain_vec, shift_vec):
    average = jnp.mean(values, axis=-1, keepdims=True)
    centred = values - average
    spread = jnp.mean(centred * centred, axis=-1, keepdims=True)
    return centred * lax.rsqrt(spread + epsilon) * gain_vec + shift_vec


def gelu_exact(values):
    return jax.nn.gelu(values, approximate=False)


def contract_rows(left, right):
    return lax.dot_general(
        left, right, (((0,), (0,)), ((), ())), preferred_element_type=jnp.float32
    )


def times_transpose(left, right):
    return lax.dot_general(
        left, right, (((1,), (1,)), ((), ())), preferred_element_type=jnp.float32
    )


def band_mask(lat_index, lat_dev, lat_total):
    wide_rows = lat_dev + 2 * ROW_REACH
    query_pos = jnp.arange(STEPS * lat_dev * LON)
    key_pos = jnp.arange(STEPS * wide_rows * LON)
    query_row = lat_index * lat_dev + query_pos // LON % lat_dev
    key_row = lat_index * lat_dev + key_pos // LON % wide_rows - ROW_REACH
    col_gap = jnp.abs((query_pos % LON)[:, None] - (key_pos % LON)[None, :])
    col_gap = jnp.minimum(col_gap, LON - col_gap)
    inside = (key_row >= 0) & (key_row < lat_total)
    row_gap = jnp.abs(query_row[:, None] - key_row[None, :])
    return inside[None, :] & (row_gap <= ROW_REACH) & (col_gap <= COL_REACH)


def body(
    tokens,
    norm1_gain,
    norm1_bias,
    qkv_weight,
    qv_bias,
    proj_weight,
    proj_bias,
    norm2_gain,
    norm2_bias,
    fc1_weight,
    fc1_bias,
    fc2_weight,
    fc2_bias,
    cotangent,
):
    items_dev, steps, lat_dev, lon_count, width = tokens.shape
    row_count = items_dev * steps * lat_dev * lon_count
    block_count = 1
    wide_rows = lat_dev + 2 * ROW_REACH
    query_len = steps * lat_dev * lon_count
    key_len = steps * wide_rows * lon_count
    score_scale = HEAD_DIM ** (-0.5)
    window = band_mask(lax.axis_index("lat"), lat_dev, lat_dev * lax.axis_size("lat"))
    band_shape = (items_dev, steps, lat_dev, lon_count, width)
    wide_shape = (items_dev, steps, wide_rows, lon_count, width)

    def masked_scores(query_blk, key_blk):
        scores = (
            jnp.einsum("bqhd,bkhd->bhqk", query_blk, key_blk, preferred_element_type=jnp.float32)
            * score_scale
        )
        return jnp.where(window, scores, -1e30)

    def forward_block(inputs):
        query_blk, key_blk, value_blk = inputs
        scores = masked_scores(query_blk, key_blk)
        row_max = jnp.max(scores, axis=-1, keepdims=True)
        shifted = jnp.exp(scores - row_max)
        exp_total = jnp.sum(shifted, axis=-1, keepdims=True)
        soft_low = (shifted / exp_total).astype(jnp.bfloat16)
        result = jnp.einsum(
            "bhqk,bkhd->bqhd", soft_low, value_blk, preferred_element_type=jnp.float32
        )
        return (result.astype(jnp.bfloat16), (row_max + jnp.log(exp_total))[..., 0])

    def backward_block(inputs):
        query_blk, key_blk, value_blk, grad_blk, log_blk = inputs
        soft_weights = jnp.exp(masked_scores(query_blk, key_blk) - log_blk[..., None])
        grad_soft = jnp.einsum(
            "bqhd,bkhd->bhqk", grad_blk, value_blk, preferred_element_type=jnp.float32
        )
        inner_sum = jnp.sum(soft_weights * grad_soft, axis=-1, keepdims=True)
        grad_scores = (soft_weights * (grad_soft - inner_sum)).astype(jnp.bfloat16)
        grad_query = (
            jnp.einsum("bhqk,bkhd->bqhd", grad_scores, key_blk, preferred_element_type=jnp.float32)
            * score_scale
        )
        grad_key = (
            jnp.einsum(
                "bhqk,bqhd->bkhd", grad_scores, query_blk, preferred_element_type=jnp.float32
            )
            * score_scale
        )
        grad_value = jnp.einsum(
            "bhqk,bqhd->bkhd",
            soft_weights.astype(jnp.bfloat16),
            grad_blk,
            preferred_element_type=jnp.float32,
        )
        return (grad_query, grad_key, grad_value)

    flat_tokens = tokens.reshape(row_count, width).astype(jnp.float32)
    normed_one, norm_one_back = jax.vjp(
        layer_norm, flat_tokens, norm1_gain.astype(jnp.float32), norm1_bias.astype(jnp.float32)
    )
    normed_low = normed_one.astype(jnp.bfloat16)
    joined_qkv = jnp.dot(normed_low, qkv_weight, preferred_element_type=jnp.float32)
    query_low = (joined_qkv[:, :width] + qv_bias[0].astype(jnp.float32)).astype(jnp.bfloat16)
    key_low = joined_qkv[:, width : 2 * width].astype(jnp.bfloat16)
    value_low = (joined_qkv[:, 2 * width :] + qv_bias[1].astype(jnp.float32)).astype(jnp.bfloat16)
    pair_kv = jnp.stack([key_low.reshape(band_shape), value_low.reshape(band_shape)])
    wide_kv = padded(pair_kv, (("lat", 3),), ROW_REACH)
    query_blocks = query_low.reshape(block_count, items_dev, query_len, HEADS, HEAD_DIM)
    wide_fwd = wide_kv.reshape(2, block_count, items_dev, key_len, HEADS, HEAD_DIM)
    attended_blocks, log_totals = lax.map(forward_block, (query_blocks, wide_fwd[0], wide_fwd[1]))
    attended_low = attended_blocks.reshape(row_count, width)
    branch = jnp.dot(
        attended_low, proj_weight, preferred_element_type=jnp.float32
    ) + proj_bias.astype(jnp.float32)
    middle = flat_tokens + branch
    normed_two, norm_two_back = jax.vjp(
        layer_norm, middle, norm2_gain.astype(jnp.float32), norm2_bias.astype(jnp.float32)
    )
    normed_two_low = normed_two.astype(jnp.bfloat16)
    hidden_pre = jnp.dot(
        normed_two_low, fc1_weight, preferred_element_type=jnp.float32
    ) + fc1_bias.astype(jnp.float32)
    hidden_act, gelu_back = jax.vjp(gelu_exact, hidden_pre)
    hidden_low = hidden_act.astype(jnp.bfloat16)
    branch_two = jnp.dot(
        hidden_low, fc2_weight, preferred_element_type=jnp.float32
    ) + fc2_bias.astype(jnp.float32)
    mixed = (middle + branch_two).astype(jnp.bfloat16).reshape(band_shape)
    cot_flat = cotangent.reshape(row_count, width)
    grad_fc2 = contract_rows(hidden_low, cot_flat)
    grad_fc2_bias = jnp.sum(cot_flat.astype(jnp.float32), axis=0)
    grad_hidden = times_transpose(cot_flat, fc2_weight)
    (grad_pre,) = gelu_back(grad_hidden)
    grad_pre_low = grad_pre.astype(jnp.bfloat16)
    grad_fc1 = contract_rows(normed_two_low, grad_pre_low)
    grad_fc1_bias = jnp.sum(grad_pre_low.astype(jnp.float32), axis=0)
    grad_normed_two = times_transpose(grad_pre_low, fc1_weight)
    grad_mid_norm, grad_gain_two, grad_bias_two = norm_two_back(grad_normed_two)
    grad_middle = cot_flat.astype(jnp.float32) + grad_mid_norm
    mlp_terms = (grad_gain_two, grad_bias_two, grad_fc1, grad_fc1_bias, grad_fc2, grad_fc2_bias)
    mlp_terms = lax.psum(
        (mlp_terms[0], mlp_terms[1], mlp_terms[2], mlp_terms[3], mlp_terms[4], mlp_terms[5]),
        ("lat", "items"),
    )
    grad_branch_low = grad_middle.astype(jnp.bfloat16)
    grad_proj = contract_rows(attended_low, grad_branch_low)
    grad_proj_bias = jnp.sum(grad_branch_low.astype(jnp.float32), axis=0)
    grad_attended_low = times_transpose(grad_branch_low, proj_weight).astype(jnp.bfloat16)
    grad_blocks = grad_attended_low.reshape(block_count, items_dev, query_len, HEADS, HEAD_DIM)
    grad_q_blocks, grad_k_blocks, grad_v_blocks = lax.map(
        backward_block, (query_blocks, wide_fwd[0], wide_fwd[1], grad_blocks, log_totals)
    )
    kv_grads = jnp.stack([grad_k_blocks.reshape(wide_shape), grad_v_blocks.reshape(wide_shape)])
    to_lower = kv_grads[:, :, :, :ROW_REACH]
    to_upper = kv_grads[:, :, :, wide_rows - ROW_REACH :]
    from_above = shifted_2(to_lower.astype(jnp.bfloat16), "lat", -1).astype(to_lower.dtype)
    from_below = shifted_2(to_upper.astype(jnp.bfloat16), "lat", 1).astype(to_upper.dtype)
    own_grads = kv_grads[:, :, :, ROW_REACH : ROW_REACH + lat_dev]
    own_grads = own_grads.at[:, :, :, :ROW_REACH].add(from_below)
    own_grads = own_grads.at[:, :, :, lat_dev - ROW_REACH :].add(from_above)
    query_grad_low = grad_q_blocks.reshape(row_count, width).astype(jnp.bfloat16)
    key_grad_low = own_grads[0].reshape(row_count, width).astype(jnp.bfloat16)
    value_grad_low = own_grads[1].reshape(row_count, width).astype(jnp.bfloat16)
    grad_joined_low = jnp.concatenate([query_grad_low, key_grad_low, value_grad_low], axis=1)
    grad_qkv = contract_rows(normed_low, grad_joined_low)
    grad_qv_bias = jnp.stack(
        [
            jnp.sum(query_grad_low.astype(jnp.float32), axis=0),
            jnp.sum(value_grad_low.astype(jnp.float32), axis=0),
        ]
    )
    grad_normed_one = times_transpose(grad_joined_low, qkv_weight)
    grad_in_norm, grad_gain_one, grad_bias_one = norm_one_back(grad_normed_one)
    tokens_grad = (grad_middle + grad_in_norm).astype(jnp.bfloat16).reshape(band_shape)
    attn_terms = (grad_gain_one, grad_bias_one, grad_qkv, grad_qv_bias, grad_proj, grad_proj_bias)
    attn_terms = lax.psum(
        (attn_terms[0], attn_terms[1], attn_terms[2], attn_terms[3], attn_terms[4], attn_terms[5]),
        ("lat", "items"),
    )
    return (
        mixed,
        tokens_grad,
        attn_terms[0],
        attn_terms[1],
        attn_terms[2],
        attn_terms[3],
        attn_terms[4],
        attn_terms[5],
        mlp_terms[0],
        mlp_terms[1],
        mlp_terms[2],
        mlp_terms[3],
        mlp_terms[4],
        mlp_terms[5],
    )


def solution(mesh):
    placed = (
        P("items", None, "lat", None, None),
        P(),
        P(),
        P(),
        P(),
        P(),
        P(),
        P(),
        P(),
        P(),
        P(),
        P(),
        P(),
        P("items", None, "lat", None, None),
    )
    return jax.shard_map(
        body,
        mesh=mesh,
        in_specs=placed,
        out_specs=(
            P("items", None, "lat", None, None),
            P("items", None, "lat", None, None),
            P(),
            P(),
            P(),
            P(),
            P(),
            P(),
            P(),
            P(),
            P(),
            P(),
            P(),
            P(),
        ),
        check_vma=False,
    )
```

profile of v0, /device:TPU:0, one launch (start us, length us, event | category | flops | bytes accessed | tf_op | source)
XLA Modules:
  0.0 365.5 jit_solution(4617219332563700692)
XLA Ops:
  7.2 1.2 convert_reduce_fusion.5
  8.5 1.1 multiply_reduce_fusion.6
  11.0 0.8 slice_convert_fusion.3
  11.9 1.1 add_convert_fusion.3
  13.0 2.0 fusion.43
  15.8 0.8 fusion.23
  16.6 3.0 collective-permute-start
  19.6 1.3 collective-permute-start.1
  22.3 2.4 collective-permute-done.1
  24.7 1.2 pad_maximum_fusion
  26.0 2.0 squeeze.37
  28.0 1.9 copy.36
  29.9 2.0 squeeze.35
  31.9 1.9 copy.37
  33.9 0.8 fusion.41
  34.7 0.9 fusion.6
  35.6 1.2 fusion.9
  36.9 1.1 copy.38
  38.0 1.5 reshape.330
  39.5 1.5 fusion.42
  41.3 2.3 convolution_add_fusion
  43.6 5.1 %convert_reduce_fusion = (f32[2048]{0:T(1024)S(1)}, bf16[192,2048]{1,0:T(8,128)(2,1)S(1)}, f32[192,2048]{1,0:T(8,128)}) fusion(f32[192,2048]{1,0:T(8,128)S(1)} %convolution_add_fusion, bf16[192,512]{1,0:T(8,128)(2,1)S(1)} %bitcast.70, bf16[2048,512]{1,0:T(8,128)(2,1)S(1)} %copy-done), kind=kOutput, calls=%fused_computation.3 | convolution fusion | flops 431749120 | bytes 6234112 | tf_op jit(solution)/shard_map/dot_general | solution.py:52
  48.7 1.0 multiply_reduce_fusion.1
  50.8 1.0 convolution_convert_fusion.1
  51.8 2.3 reshape.338
  54.1 2.5 copy.40
  56.6 3.2 convolution_bitcast_fusion
  59.7 1.5 multiply_reduce_fusion
  61.2 1.0 multiply_convert_fusion
  62.2 1.3 convert_reduce_fusion.1
  63.5 1.2 fusion.7
  64.7 3.1 copy.45
  67.9 2.7 stack_reshape.14
  70.5 1.0 constant_dynamic-update-slice_fusion.1
  71.5 3.1 copy.47
  74.6 2.7 stack_reshape.15
  77.3 1.0 constant_dynamic-update-slice_fusion
  78.2 2.6 convert.14
  80.8 0.9 slice.152
  81.7 2.9 fusion.35
  84.8 0.8 copy-done.26
  85.6 1.1 copy.43
  86.7 2.1 convert_element_type.163
  88.8 1.0 fusion.39
  89.9 1.3 collective-permute-start.3
  91.2 6.8 %collective-permute-start.2 = (bf16[2,3,2,1,16,512]{5,4,3,2,1,0:T(8,128)(2,1)S(1)}, bf16[2,3,2,1,16,512]{5,4,3,2,1,0:T(8,128)(2,1)S(1)}, u32[]{:S(2)}, u32[]{:S(2)}) collective-permute-start(bf16[2,3,2,1,16,512]{5,4,3,2,1,0:T(8,128)(2,1)S(1)} %get-tuple-element.119), channel_id=1, source_target_pairs={{0,8},{8,16},{16,24},{1,9},{9,17},{17,25},{2,10},{10,18},{18,26},{... | collective-permute-start | bytes 589832 | tf_op jit(solution)/shard_map/ppermute | solution.py:31
  98.0 3.7 %fusion.45 = f32[2048,512]{1,0:T(8,128)} fusion(bf16[192,2048]{1,0:T(8,128)(2,1)S(1)} %multiply_convert_fusion.1, bf16[192,512]{1,0:T(8,128)(2,1)} %bitcast.69), kind=kOutput, calls=%fused_computation.130 | convolution fusion | flops 402653184 | bytes 5177344 | tf_op jit(solution)/shard_map/dot_general | solution.py:46
  101.7 1.3 fusion.44
  103.0 1.1 fusion.17
  104.9 0.7 convert_reduce_fusion.4
  105.6 1.8 copy.48
  107.4 1.8 copy.49
  109.1 3.5 fusion.20
  113.3 1.0 convert_reduce_fusion.2
  114.4 1.3 fusion.13
  116.0 0.8 multiply_reduce_fusion.2
  117.2 43.1 %all-reduce = (f32[512]{0:T(512)}, f32[512]{0:T(512)}, f32[2,512]{1,0:T(2,128)}, f32[512]{0:T(512)}, f32[512]{0:T(512)}, /*index=5*/f32[512]{0:T(512)}, f32[2048]{0:T(1024)}, f32[512]{0:T(512)}) all-reduce(f32[512]{0:T(512)S(1)} %get-tuple-element.91, ...), channel_id=1, replica_groups=mesh['lat'=4,'items'=8] {'lat','items'}, use_global_device_ids=true, to_apply=%region_12.13 | all-reduce | flops 6144 | bytes 49152 | tf_op jit(solution)/shard_map/psum | solution.py:221
  160.3 0.8 add_convert_fusion.1
  161.1 186.9 %all-reduce.4.cloned.1.call-done = (f32[512,1536]{1,0:T(8,128)}, f32[512,512]{1,0:T(8,128)}, f32[512,2048]{1,0:T(8,128)}, f32[2048,512]{1,0:T(8,128)}) async-done(((f32[512,1536]{1,0:T(8,128)}, f32[512,512]{1,0:T(8,128)}, f32[512,2048]{1,0:T(8,128)}, f32[2048,512]{1,0:T(8,128)}), (f32[512,1536]{1,0:T(8,128)}, f32[512,512]{1,0:T(8,128)}, f32[512,2048]{1,0:T(8,128)}, ...) | async-done | bytes 12582928 | tf_op jit(solution)/shard_map/psum | solution.py:221
  348.0 3.9 %copy.61 = f32[512,1536]{1,0:T(8,128)} copy(f32[512,1536]{1,0:T(8,128)} %get-tuple-element.144) | data formatting | bytes 6291456
  351.9 1.0 copy.62
  352.9 2.1 copy.63
  355.1 1.6 copy-done.7
  356.6 2.0 copy.64
  (123 shorter events, 7.6 us)
Async XLA Ops:
  7.2 36.4 %copy-start = (bf16[2048,512]{1,0:T(8,128)(2,1)S(1)}, bf16[2048,512]{1,0:T(8,128)(2,1)}, u32[]{:S(2)}) copy-start(bf16[2048,512]{1,0:T(8,128)(2,1)} %param.29) | copy-start | bytes 6291460
  7.2 340.8 %all-reduce.4.cloned.1.call-start = ((), (), s32[]{:S(2)}) async-start(), calls=%async_computation | async-start | bytes 25165824 | tf_op jit(solution)/shard_map/psum | solution.py:221
  13.0 2.1 copy-start.21
  14.9 6.0 %copy-start.37 = (bf16[512]{0:T(512)(128)(2,1)S(1)}, bf16[512]{0:T(512)(128)(2,1)}, u32[]{:S(2)}) copy-start(bf16[512]{0:T(512)(128)(2,1)} %param.25) | copy-start | bytes 3076
  15.0 6.0 %copy-start.38 = (bf16[512]{0:T(512)(128)(2,1)S(1)}, bf16[512]{0:T(512)(128)(2,1)}, u32[]{:S(2)}) copy-start(bf16[512]{0:T(512)(128)(2,1)} %param.26) | copy-start | bytes 3076
  15.0 6.0 %copy-start.39 = (bf16[512]{0:T(512)(128)(2,1)S(1)}, bf16[512]{0:T(512)(128)(2,1)}, u32[]{:S(2)}) copy-start(bf16[512]{0:T(512)(128)(2,1)} %param.24) | copy-start | bytes 3076
  15.0 6.1 %copy-start.36 = (bf16[2048]{0:T(1024)(128)(2,1)S(1)}, bf16[2048]{0:T(1024)(128)(2,1)}, u32[]{:S(2)}) copy-start(bf16[2048]{0:T(1024)(128)(2,1)} %param.28) | copy-start | bytes 12292
  15.1 0.7 copy-start.22
  16.6 5.7 %collective-permute-start = (bf16[2,3,2,1,16,512]{5,4,3,2,1,0:T(8,128)(2,1)}, bf16[2,3,2,1,16,512]{5,4,3,2,1,0:T(8,128)(2,1)}, u32[]{:S(2)}, u32[]{:S(2)}) collective-permute-start(bf16[2,3,2,1,16,512]{5,4,3,2,1,0:T(8,128)(2,1)} %get-tuple-element.122), channel_id=1, source_target_pairs={{0,8},{8,16},{16,24},{1,9},{9,17},{17,25},{2,10},{10,18},{18,26},{... | collective-permute-start | bytes 589832 | tf_op jit(solution)/shard_map/ppermute | solution.py:20
  19.6 5.1 %collective-permute-start.1 = (bf16[2,3,2,1,16,512]{5,4,3,2,1,0:T(8,128)(2,1)}, bf16[2,3,2,1,16,512]{5,4,3,2,1,0:T(8,128)(2,1)}, u32[]{:S(2)}, u32[]{:S(2)}) collective-permute-start(bf16[2,3,2,1,16,512]{5,4,3,2,1,0:T(8,128)(2,1)} %get-tuple-element.123), channel_id=1, source_target_pairs={{8,0},{16,8},{24,16},{9,1},{17,9},{25,17},{10,2},{18,10},{26,18},{... | collective-permute-start | bytes 589832 | tf_op jit(solution)/shard_map/ppermute | solution.py:23
  29.9 3.9 %copy-start.11 = (bf16[3,128,16,32]{1,3,2,0:T(8,128)(2,1)}, bf16[3,128,16,32]{1,3,2,0:T(8,128)(2,1)S(1)}, u32[]{:S(2)}) copy-start(bf16[3,128,16,32]{1,3,2,0:T(8,128)(2,1)S(1)} %copy.36) | copy-start | bytes 1179652
  33.9 1.7 copy-start.28
  34.7 2.2 copy-start.1
  36.8 2.7 copy-start.6
  39.5 4.1 %copy-start.17 = (bf16[192,512]{0,1:T(8,128)(2,1)}, bf16[192,512]{0,1:T(8,128)(2,1)S(1)}, u32[]{:S(2)}) copy-start(bf16[192,512]{0,1:T(8,128)(2,1)S(1)} %reshape.330) | copy-start | bytes 589828
  41.3 2.3 copy-start.14
  43.6 5.1 %copy-start.4 = (f32[192,2048]{1,0:T(8,128)}, f32[192,2048]{1,0:T(8,128)S(1)}, u32[]{:S(2)}) copy-start(f32[192,2048]{1,0:T(8,128)S(1)} %convolution_add_fusion) | copy-start | bytes 4718596
  43.6 5.1 %copy-start.20 = (bf16[512,2048]{1,0:T(8,128)(2,1)S(1)}, bf16[512,2048]{1,0:T(8,128)(2,1)}, u32[]{:S(2)}) copy-start(bf16[512,2048]{1,0:T(8,128)(2,1)} %param.27) | copy-start | bytes 6291460
  48.7 1.0 copy-start.34
  49.7 1.1 copy-start.19
  50.0 6.6 %copy-start.9 = (f32[192,512]{1,0:T(8,128)}, f32[192,512]{1,0:T(8,128)S(1)}, u32[]{:S(2)}) copy-start(f32[192,512]{1,0:T(8,128)S(1)} %get-tuple-element.115) | copy-start | bytes 1179652
  50.1 0.7 copy-start.23
  56.6 3.2 copy-start.2
  56.6 3.2 copy-start.13
  56.6 3.2 copy-start.29
  61.2 1.0 copy-start.12
  78.2 2.6 copy-start.3
  78.2 3.5 copy-start.35
  81.7 2.9 copy-start.5
  81.7 2.9 copy-start.27
  84.6 1.0 copy-start.26
  89.9 14.2 %collective-permute-start.3 = (bf16[2,3,2,1,16,512]{5,4,3,2,1,0:T(8,128)(2,1)S(1)}, bf16[2,3,2,1,16,512]{5,4,3,2,1,0:T(8,128)(2,1)S(1)}, u32[]{:S(2)}, u32[]{:S(2)}) collective-permute-start(bf16[2,3,2,1,16,512]{5,4,3,2,1,0:T(8,128)(2,1)S(1)} %get-tuple-element.118), channel_id=1, source_target_pairs={{8,0},{16,8},{24,16},{9,1},{17,9},{25,17},{10,2},{18,10},{26,18},{... | collective-permute-start | bytes 589832 | tf_op jit(solution)/shard_map/ppermute | solution.py:31
  91.2 10.5 %copy-start.18 = (bf16[192,512]{0,1:T(8,128)(2,1)S(1)}, bf16[192,512]{0,1:T(8,128)(2,1)}, u32[]{:S(2)}) copy-start(bf16[192,512]{0,1:T(8,128)(2,1)} %copy-done.17) | copy-start | bytes 589828
  91.2 10.5 %copy-start.24 = (bf16[192,512]{1,0:T(8,128)(2,1)S(1)}, bf16[192,512]{1,0:T(8,128)(2,1)}, u32[]{:S(2)}) copy-start(bf16[192,512]{1,0:T(8,128)(2,1)} %copy-done.23) | copy-start | bytes 589828
  91.2 11.8 %copy-start.16 = (f32[2,3,2,2,16,512]{5,4,3,2,1,0:T(8,128)S(1)}, f32[2,3,2,2,16,512]{5,4,3,2,1,0:T(8,128)}, u32[]{:S(2)}) copy-start(f32[2,3,2,2,16,512]{5,4,3,2,1,0:T(8,128)} %slice.152) | copy-start | bytes 2359300
  91.2 11.8 %collective-permute-start.2 = (bf16[2,3,2,1,16,512]{5,4,3,2,1,0:T(8,128)(2,1)S(1)}, bf16[2,3,2,1,16,512]{5,4,3,2,1,0:T(8,128)(2,1)S(1)}, u32[]{:S(2)}, u32[]{:S(2)}) collective-permute-start(bf16[2,3,2,1,16,512]{5,4,3,2,1,0:T(8,128)(2,1)S(1)} %get-tuple-element.119), channel_id=1, source_target_pairs={{0,8},{8,16},{16,24},{1,9},{9,17},{17,25},{2,10},{10,18},{18,26},{... | collective-permute-start | bytes 589832 | tf_op jit(solution)/shard_map/ppermute | solution.py:31
  112.6 0.7 copy-start.40
  114.4 1.4 copy-start.25
  114.4 1.4 copy-start.30
  114.4 1.5 copy-start.31
  114.4 1.6 copy-start.32
  116.8 43.4 %copy-start.10 = (f32[192,512]{1,0:T(8,128)S(1)}, f32[192,512]{1,0:T(8,128)}, u32[]{:S(2)}) copy-start(f32[192,512]{1,0:T(8,128)} %copy-done.9) | copy-start | bytes 1179652
  116.8 43.4 %copy-start.15 = (bf16[3,2,2,16,512]{4,3,2,1,0:T(8,128)(2,1)S(1)}, bf16[3,2,2,16,512]{4,3,2,1,0:T(8,128)(2,1)}, u32[]{:S(2)}) copy-start(bf16[3,2,2,16,512]{4,3,2,1,0:T(8,128)(2,1)} %param.31) | copy-start | bytes 589828
  348.0 3.9 %copy-start.33 = (f32[512,512]{1,0:T(8,128)S(1)}, f32[512,512]{1,0:T(8,128)}, u32[]{:S(2)}) copy-start(f32[512,512]{1,0:T(8,128)} %get-tuple-element.146) | copy-start | bytes 3145732
  348.0 4.9 %copy-start.8 = (f32[512,2048]{1,0:T(8,128)S(1)}, f32[512,2048]{1,0:T(8,128)}, u32[]{:S(2)}) copy-start(f32[512,2048]{1,0:T(8,128)} %get-tuple-element.150) | copy-start | bytes 12582916
  352.9 3.7 %copy-start.7 = (f32[2048,512]{1,0:T(8,128)S(1)}, f32[2048,512]{1,0:T(8,128)}, u32[]{:S(2)}) copy-start(f32[2048,512]{1,0:T(8,128)} %get-tuple-element.152) | copy-start | bytes 12582916
Sparse Core Ops, SparseCore 0:
  112.8 235.1 all-reduce.3
where the time goes:
time: 367 us; the launch traced here: 365 us
  waiting for transfers between devices  189 us (51%)
  local copies, waits for them, and re-layouts  53.5 us (15%)
  blocking collectives  43.1 us (12%)
  matrix products  35.3 us (10%)
  other arithmetic  17 us (5%)
  between operations  14.7 us (4%)
  starting transfers between devices  12.5 us (3%)
    psum x1, waiting for transfers between devices, body(): lax.psum((attn_terms[0], attn_terms[1], attn_terms[2], attn_terms[3], att...  187 us
    psum x1, blocking collectives, body(): lax.psum((attn_terms[0], attn_terms[1], attn_terms[2], attn_terms[3], att...  43.1 us
    unnamed x87, local copies, waits for them, and re-layouts  14.9 us
    squeeze x8, local copies, waits for them, and re-layouts, body(): lax.map(forward_block, (query_blocks, wide_fwd[0], wide_fwd[1]))  13.6 us
    dot_general x4, matrix products, contract_rows(): lax.dot_general(left, right, (((0,), (0,)), ((), ())), preferred_element_...  11.3 us
    ppermute x2, starting transfers between devices, shifted_2(): return lax.ppermute(block, axis, route)  8.09 us
    dot_general x4, matrix products, times_transpose(): lax.dot_general(left, right, (((1,), (1,)), ((), ())), preferred_element_...  7.89 us
  transfers between devices with their start and end apart: 5, of which 2 were waited for; matrix products, arithmetic and copies ran while one was open for 3% of the time, Pallas kernels for 0%

commit v1 on v0

--- a/solution.py
+++ b/solution.py
@@ -219,8 +219,18 @@
     tokens_grad = (grad_middle + grad_in_norm).astype(jnp.bfloat16).reshape(band_shape)
     attn_terms = (grad_gain_one, grad_bias_one, grad_qkv, grad_qv_bias, grad_proj, grad_proj_bias)
     attn_terms = lax.psum(
-        (attn_terms[0], attn_terms[1], attn_terms[2], attn_terms[3], attn_terms[4], attn_terms[5]),
-        ("lat", "items"),
+        lax.psum(
+            (
+                attn_terms[0],
+                attn_terms[1],
+                attn_terms[2],
+                attn_terms[3],
+                attn_terms[4],
+                attn_terms[5],
+            ),
+            "items",
+        ),
+        "lat",
     )
     return (
         mixed,

time: 367 us -> 557 us (1.52)
  waiting for transfers between devices: 189 us -> 334 us
  blocking collectives: 43.1 us -> 89.9 us
    psum x0 -> x2, waiting for transfers between devices: none -> 179 us  [the longest x1 90.6 us: body(): lax.psum((mlp_terms[0], mlp_terms[1], mlp_terms[2], mlp_terms[3], mlp_ter...]
    psum x0 -> x2, blocking collectives: none -> 51.9 us  [the longest x1 41.1 us: body(): lax.psum((mlp_terms[0], mlp_terms[1], mlp_terms[2], mlp_terms[3], mlp_ter...]
    psum x1, waiting for transfers between devices: 187 us -> 153 us  [body(): lax.psum((attn_terms[0], attn_terms[1], attn_terms[2], attn_terms[3], att...]
    unnamed x87 -> x83, local copies, waits for them, and re-layouts: 14.9 us -> 14.1 us
  transfers between devices with their start and end apart: 5 -> 7, of which waited for: 2 -> 4; matrix products, arithmetic and copies ran while one was open for 3% -> 3% of each run, Pallas kernels for 0% -> 0%
where the time goes in v1:
time: 557 us; the launch traced here: 556 us
  waiting for transfers between devices  334 us (60%)
  blocking collectives  89.9 us (16%)
  local copies, waits for them, and re-layouts  50.5 us (9%)
  matrix products  35.4 us (6%)
  other arithmetic  18.9 us (3%)
  between operations  14.5 us (3%)
  starting transfers between devices  12.4 us (2%)
    psum x1, waiting for transfers between devices, body(): lax.psum((attn_terms[0], attn_terms[1], attn_terms[2], attn_terms[3], att...  153 us
    psum x1, waiting for transfers between devices, body(): lax.psum((mlp_terms[0], mlp_terms[1], mlp_terms[2], mlp_terms[3], mlp_ter...  90.6 us
    psum x1, waiting for transfers between devices, body(): lax.psum(lax.psum((attn_terms[0], attn_terms[1], attn_terms[2], attn_term...  88.2 us
    psum x1, blocking collectives, body(): lax.psum((mlp_terms[0], mlp_terms[1], mlp_terms[2], mlp_terms[3], mlp_ter...  41.1 us
    psum x1, blocking collectives, body(): lax.psum((attn_terms[0], attn_terms[1], attn_terms[2], attn_terms[3], att...  38 us
    unnamed x83, local copies, waits for them, and re-layouts  14.1 us
    squeeze x8, local copies, waits for them, and re-layouts, body(): lax.map(forward_block, (query_blocks, wide_fwd[0], wide_fwd[1]))  13.6 us
    dot_general x4, matrix products, contract_rows(): lax.dot_general(left, right, (((0,), (0,)), ((), ())), preferred_element_...  11.3 us
  transfers between devices with their start and end apart: 7, of which 4 were waited for; matrix products, arithmetic and copies ran while one was open for 3% of the time, Pallas kernels for 0%

profile of v1, /device:TPU:0, one launch (start us, length us, event | category | flops | bytes accessed | tf_op | source)
XLA Modules:
  0.0 555.9 jit_solution(13286199130329647680)
XLA Ops:
  7.2 1.2 convert_reduce_fusion.5
  8.5 1.1 multiply_reduce_fusion.6
  11.9 1.1 add_convert_fusion.3
  13.0 2.0 fusion.43
  15.8 0.8 fusion.23
  16.6 3.0 collective-permute-start
  19.6 1.3 collective-permute-start.1
  22.3 2.5 collective-permute-done.1
  24.7 1.2 pad_maximum_fusion
  26.0 2.0 squeeze.37
  28.0 1.9 copy.36
  29.9 2.0 squeeze.35
  32.0 1.9 copy.37
  34.7 0.9 fusion.6
  35.6 1.2 fusion.9
  36.9 1.1 copy.38
  38.0 1.5 reshape.330
  39.5 1.5 fusion.42
  41.3 2.3 convolution_add_fusion
  43.6 5.1 convert_reduce_fusion
  48.7 1.0 multiply_reduce_fusion.1
  50.8 1.0 convolution_convert_fusion.1
  51.8 2.3 reshape.338
  54.1 2.4 copy.40
  56.6 3.2 convolution_bitcast_fusion
  59.7 1.5 multiply_reduce_fusion
  61.2 1.0 multiply_convert_fusion
  62.3 1.3 convert_reduce_fusion.1
  63.5 1.2 fusion.7
  64.7 3.1 copy.45
  67.9 2.7 stack_reshape.14
  70.5 0.9 constant_dynamic-update-slice_fusion.1
  71.5 3.1 copy.47
  74.6 2.7 stack_reshape.15
  77.3 1.0 constant_dynamic-update-slice_fusion
  78.2 2.6 convert.14
  80.9 1.1 copy.43
  82.0 2.1 convert_element_type.163
  84.1 1.0 fusion.39
  85.2 1.3 collective-permute-start.3
  86.5 6.7 %collective-permute-start.2 = (bf16[2,3,2,1,16,512]{5,4,3,2,1,0:T(8,128)(2,1)S(1)}, bf16[2,3,2,1,16,512]{5,4,3,2,1,0:T(8,128)(2,1)S(1)}, u32[]{:S(2)}, u32[]{:S(2)}) collective-permute-start(bf16[2,3,2,1,16,512]{5,4,3,2,1,0:T(8,128)(2,1)S(1)} %get-tuple-element.125), channel_id=1, source_target_pairs={{0,8},{8,16},{16,24},{1,9},{9,17},{17,25},{2,10},{10,18},{18,26},{... | collective-permute-start | bytes 589832 | tf_op jit(solution)/shard_map/ppermute | solution.py:31
  93.2 2.3 fusion.44
  95.4 1.1 fusion.17
  98.0 1.1 copy.48
  99.1 1.2 copy.49
  100.3 3.4 fusion.20
  103.8 2.1 multiply_convert_fusion.1
  106.0 2.8 fusion.45
  108.7 2.9 fusion.35
  111.7 153.0 %all-reduce.12.cloned.1.call-done = (f32[512,1536]{1,0:T(8,128)}, f32[512,512]{1,0:T(8,128)}) async-done(((f32[512,1536]{1,0:T(8,128)}, f32[512,512]{1,0:T(8,128)}), (f32[512,1536]{1,0:T(8,128)}, f32[512,512]{1,0:T(8,128)})) %all-reduce.12.cloned.1.call-update) | async-done | bytes 4194320 | tf_op jit(solution)/shard_map/psum | solution.py:222
  265.4 1.0 convert_reduce_fusion.2
  266.4 41.1 %all-reduce = (f32[512]{0:T(512)}, f32[512]{0:T(512)}, f32[2048]{0:T(1024)}, f32[512]{0:T(512)}) all-reduce(f32[512]{0:T(512)S(1)} %get-tuple-element.89, f32[512]{0:T(512)S(1)} %get-tuple-element.93, f32[2048]{0:T(1024)S(1)} %get-tuple-element.113, f32[512]{0:T(512)S(1)} %convert_reduce_fusion.2), channel_id=1, replica_groups=mesh['lat'=4,'items'=8] {'lat','items'}, use_global_device_ids=true, to_apply=%region_29.30 | all-reduce | flops 3584 | bytes 28672 | tf_op jit(solution)/shard_map/psum | solution.py:186
  307.5 1.3 fusion.13
  309.2 0.8 multiply_reduce_fusion.2
  310.4 38.0 %all-reduce.2 = (f32[512]{0:T(512)S(1)}, f32[512]{0:T(512)S(1)}, f32[2,512]{1,0:T(2,128)S(1)}, f32[512]{0:T(512)S(1)}) all-reduce(f32[512]{0:T(512)S(1)} %get-tuple-element.91, f32[512]{0:T(512)S(1)} %get-tuple-element.94, f32[2,512]{1,0:T(2,128)S(1)} %pad_maximum_fusion.5, ...), channel_id=1, replica_groups=mesh['lat'=4,'items'=8] {'items'}, use_global_device_ids=true, to_apply=%region_12.13 | all-reduce | flops 2560 | bytes 20480 | tf_op jit(solution)/shard_map/psum | solution.py:222
  348.3 10.8 %all-reduce.4 = (f32[512]{0:T(512)}, f32[512]{0:T(512)}, f32[2,512]{1,0:T(2,128)}, f32[512]{0:T(512)}) all-reduce(f32[512]{0:T(512)S(1)} %get-tuple-element.101, f32[512]{0:T(512)S(1)} %get-tuple-element.102, f32[2,512]{1,0:T(2,128)S(1)} %get-tuple-element.103, ...), channel_id=1, replica_groups=mesh['lat'=4,'items'=8] {'lat'}, use_global_device_ids=true, to_apply=%region_13.14 | all-reduce | flops 2560 | bytes 20480 | tf_op jit(solution)/shard_map/psum | solution.py:221
  359.2 0.8 add_convert_fusion.1
  360.0 90.6 %all-reduce.10.cloned.1.call-done = (f32[512,2048]{1,0:T(8,128)}, f32[2048,512]{1,0:T(8,128)}) async-done(((f32[512,2048]{1,0:T(8,128)}, f32[2048,512]{1,0:T(8,128)}), (f32[512,2048]{1,0:T(8,128)}, f32[2048,512]{1,0:T(8,128)})) %all-reduce.10.cloned.1.call-update) | async-done | bytes 8388624 | tf_op jit(solution)/shard_map/psum | solution.py:186
  450.6 88.2 %all-reduce.14.cloned.1.call-done = (f32[512,1536]{1,0:T(8,128)}, f32[512,512]{1,0:T(8,128)}) async-done(((f32[512,1536]{1,0:T(8,128)}, f32[512,512]{1,0:T(8,128)}), (f32[512,1536]{1,0:T(8,128)}, f32[512,512]{1,0:T(8,128)})) %all-reduce.14.cloned.1.call-update) | async-done | bytes 4194320 | tf_op jit(solution)/shard_map/psum | solution.py:221
  538.8 3.9 copy.63
  542.7 1.0 copy.64
  543.7 2.1 copy.65
  545.8 1.6 copy-done.6
  547.4 2.0 copy.66
  (127 shorter events, 9.8 us)
Async XLA Ops:
  7.2 36.4 %copy-start = (bf16[2048,512]{1,0:T(8,128)(2,1)S(1)}, bf16[2048,512]{1,0:T(8,128)(2,1)}, u32[]{:S(2)}) copy-start(bf16[2048,512]{1,0:T(8,128)(2,1)} %param.29) | copy-start | bytes 6291460
  7.2 257.5 %all-reduce.12.cloned.1.call-start = ((), (), s32[]{:S(2)}) async-start(), calls=%async_computation.1 | async-start | bytes 8388608 | tf_op jit(solution)/shard_map/psum | solution.py:222
  13.0 2.1 copy-start.19
  15.0 6.0 %copy-start.35 = (bf16[512]{0:T(512)(128)(2,1)S(1)}, bf16[512]{0:T(512)(128)(2,1)}, u32[]{:S(2)}) copy-start(bf16[512]{0:T(512)(128)(2,1)} %param.25) | copy-start | bytes 3076
  15.0 6.0 %copy-start.36 = (bf16[512]{0:T(512)(128)(2,1)S(1)}, bf16[512]{0:T(512)(128)(2,1)}, u32[]{:S(2)}) copy-start(bf16[512]{0:T(512)(128)(2,1)} %param.26) | copy-start | bytes 3076
  15.0 6.0 %copy-start.37 = (bf16[512]{0:T(512)(128)(2,1)S(1)}, bf16[512]{0:T(512)(128)(2,1)}, u32[]{:S(2)}) copy-start(bf16[512]{0:T(512)(128)(2,1)} %param.24) | copy-start | bytes 3076
  15.0 6.0 %copy-start.34 = (bf16[2048]{0:T(1024)(128)(2,1)S(1)}, bf16[2048]{0:T(1024)(128)(2,1)}, u32[]{:S(2)}) copy-start(bf16[2048]{0:T(1024)(128)(2,1)} %param.28) | copy-start | bytes 12292
  15.1 0.7 copy-start.20
  16.6 5.7 %collective-permute-start = (bf16[2,3,2,1,16,512]{5,4,3,2,1,0:T(8,128)(2,1)}, bf16[2,3,2,1,16,512]{5,4,3,2,1,0:T(8,128)(2,1)}, u32[]{:S(2)}, u32[]{:S(2)}) collective-permute-start(bf16[2,3,2,1,16,512]{5,4,3,2,1,0:T(8,128)(2,1)} %get-tuple-element.128), channel_id=1, source_target_pairs={{0,8},{8,16},{16,24},{1,9},{9,17},{17,25},{2,10},{10,18},{18,26},{... | collective-permute-start | bytes 589832 | tf_op jit(solution)/shard_map/ppermute | solution.py:20
  19.6 5.1 collective-permute-start.1
  29.9 3.9 copy-start.10
  33.9 1.7 copy-start.24
  34.7 2.2 copy-start.1
  36.9 2.7 copy-start.5
  39.5 4.1 copy-start.16
  41.3 2.3 copy-start.13
  43.6 5.1 copy-start.4
  43.6 5.1 copy-start.18
  48.7 1.0 copy-start.32
  49.7 1.1 copy-start.17
  50.0 6.6 %copy-start.8 = (f32[192,512]{1,0:T(8,128)}, f32[192,512]{1,0:T(8,128)S(1)}, u32[]{:S(2)}) copy-start(f32[192,512]{1,0:T(8,128)S(1)} %get-tuple-element.121) | copy-start | bytes 1179652
  50.2 0.7 copy-start.21
  56.5 3.2 copy-start.2
  56.5 3.2 copy-start.12
  56.5 3.2 copy-start.25
  61.2 1.0 copy-start.11
  78.2 2.6 copy-start.3
  78.2 2.6 copy-start.23
  85.2 11.3 %collective-permute-start.3 = (bf16[2,3,2,1,16,512]{5,4,3,2,1,0:T(8,128)(2,1)S(1)}, bf16[2,3,2,1,16,512]{5,4,3,2,1,0:T(8,128)(2,1)S(1)}, u32[]{:S(2)}, u32[]{:S(2)}) collective-permute-start(bf16[2,3,2,1,16,512]{5,4,3,2,1,0:T(8,128)(2,1)S(1)} %get-tuple-element.124), channel_id=1, source_target_pairs={{8,0},{16,8},{24,16},{9,1},{17,9},{25,17},{10,2},{18,10},{26,18},{... | collective-permute-start | bytes 589832 | tf_op jit(solution)/shard_map/ppermute | solution.py:31
  86.5 8.9 %collective-permute-start.2 = (bf16[2,3,2,1,16,512]{5,4,3,2,1,0:T(8,128)(2,1)S(1)}, bf16[2,3,2,1,16,512]{5,4,3,2,1,0:T(8,128)(2,1)S(1)}, u32[]{:S(2)}, u32[]{:S(2)}) collective-permute-start(bf16[2,3,2,1,16,512]{5,4,3,2,1,0:T(8,128)(2,1)S(1)} %get-tuple-element.125), channel_id=1, source_target_pairs={{0,8},{8,16},{16,24},{1,9},{9,17},{17,25},{2,10},{10,18},{18,26},{... | collective-permute-start | bytes 589832 | tf_op jit(solution)/shard_map/ppermute | solution.py:31
  99.1 4.6 copy-start.27
  100.3 3.5 copy-start.29
  103.7 346.9 %all-reduce.10.cloned.1.call-start = ((), (), s32[]{:S(2)}) async-start(), calls=%async_computation | async-start | bytes 16777216 | tf_op jit(solution)/shard_map/psum | solution.py:186
  103.8 2.2 copy-start.14
  105.9 2.8 copy-start.33
  111.6 427.2 %all-reduce.14.cloned.1.call-start = ((), (), s32[]{:S(2)}) async-start(), calls=%async_computation.2 | async-start | bytes 8388608 | tf_op jit(solution)/shard_map/psum | solution.py:221
  264.7 0.7 copy-start.38
  307.5 1.4 copy-start.22
  307.5 1.4 copy-start.26
  307.5 1.6 copy-start.28
  307.5 1.7 copy-start.30
  310.0 49.1 %copy-start.9 = (f32[192,512]{1,0:T(8,128)S(1)}, f32[192,512]{1,0:T(8,128)}, u32[]{:S(2)}) copy-start(f32[192,512]{1,0:T(8,128)} %copy-done.8) | copy-start | bytes 1179652
  310.0 49.1 %copy-start.15 = (bf16[3,2,2,16,512]{4,3,2,1,0:T(8,128)(2,1)S(1)}, bf16[3,2,2,16,512]{4,3,2,1,0:T(8,128)(2,1)}, u32[]{:S(2)}) copy-start(bf16[3,2,2,16,512]{4,3,2,1,0:T(8,128)(2,1)} %param.31) | copy-start | bytes 589828
  538.8 3.9 copy-start.31
  538.8 4.9 copy-start.7
  543.7 3.7 copy-start.6
Sparse Core Ops, SparseCore 0:
  103.8 160.7 all-reduce.11
  271.1 179.4 all-reduce.9
  453.0 85.7 all-reduce.13
